TPU v7x, 32 devices: a whole 2x2x4 slice. The times are simulated.
32 devices in a mesh: ctx: 8 (over z, core), tp: 4 (over y, x).
Axes of the slice: x: 2, y: 2, z: 4, core: 2. Of those that a mesh axis runs over, the one named last changes fastest.
Arguments:
- queries: bfloat16 [2048, 8192], P('ctx', 'tp'), may hold values from -6 to 6
- keys: bfloat16 [2048, 8192], P('ctx', 'tp'), may hold values from -0.125 to 0.125
- values: bfloat16 [2048, 8192], P('ctx', 'tp'), may hold values from -6 to 6
- log_keep: float32 [64, 2048], P('tp', 'ctx'), may hold values from -1 to 0, as said below
- state_in: float32 [64, 128, 128], P('tp'), may hold values from -6 to 6
- norm_gain: float32 [8192], P('tp'), may hold values from 0.1 to 1.9
- out_weight: bfloat16 [8192, 6144], P('tp', 'ctx'), may hold values from -0.09375 to 0.09375
Outputs:
- normed: bfloat16 [2048, 8192], P('ctx', 'tp')
- state_out: float32 [64, 128, 128], P('tp', 'ctx')
- layer_out: bfloat16 [2048, 6144], P('ctx', 'tp')
Inputs may be any that keep to these rules, and one draw needn't show every extreme that they name: `log_keep`: every entry is a logarithm of a keep factor, so at most 0.
All inputs are finite; a program needn't handle non-finite values.
Results may differ from a plain program's by a relative error of at most 0.014.
Values may be sent and summed in bfloat16 or wider, within the bound.
A program may use at most 128 MiB of HBM per device.

v0:
```python
import jax
import jax.numpy as jnp
from jax import lax
from jax.sharding import PartitionSpec as P

H = 64
DH = 128
SPAN = 256


HIGH = lax.Precision.HIGHEST
EPSILON = 1e-06


def shifted(x, axis, by):
    peers = lax.axis_size(axis)
    pairs = [(i, i + by) for i in range(peers) if 0 <= i + by < peers]
    return lax.ppermute(x, axis, pairs)


def broadcast(x, axis, root):
    mine = lax.axis_index(axis) == root
    return lax.psum(jnp.where(mine, x, jnp.zeros_like(x)), axis)


def join_states(earlier, later):
    log_early, state_early = earlier
    log_late, state_late = later
    return (log_early + log_late, jnp.exp(log_late)[:, None, None] * state_early + state_late)


def close_chain(prev_log, prev_state, own_log, own_state, state_in):
    last_log, last_state = join_states((prev_log, prev_state), (own_log, own_state))
    return jnp.exp(last_log)[:, None, None] * state_in + last_state


def per_device(queries, keys, values, log_keep, state_in, norm_gain, out_weight):
    tokens_here = queries.shape[0]
    heads = log_keep.shape[0]
    width = state_in.shape[1]
    blocks = tokens_here // SPAN
    q_blocks = queries.reshape(blocks, SPAN, heads, width)
    k_blocks = keys.reshape(blocks, SPAN, heads, width)
    v_blocks = values.reshape(blocks, SPAN, heads, width)
    within = jnp.cumsum(log_keep.reshape(heads, blocks, SPAN), axis=2)
    causal = jnp.tril(jnp.ones((SPAN, SPAN), dtype=bool))
    spread = within[:, :, :, None] - within[:, :, None, :]
    decay = jnp.where(causal, jnp.exp(jnp.minimum(spread, 0.0)), 0.0)
    scores = jnp.einsum("cshd,cthd->hcst", q_blocks, k_blocks, preferred_element_type=jnp.float32)
    weights = (scores * decay).astype(jnp.bfloat16)
    intra = jnp.einsum("hcst,cthd->cshd", weights, v_blocks, preferred_element_type=jnp.float32)
    block_log = within[:, :, -1]
    key_factor = jnp.exp(block_log[:, :, None] - within).transpose(1, 2, 0)
    keys_decayed = (k_blocks * key_factor[:, :, :, None]).astype(jnp.bfloat16)
    increments = jnp.einsum(
        "cshd,cshe->chde", keys_decayed, v_blocks, preferred_element_type=jnp.float32
    )
    running = jnp.cumsum(block_log, axis=1)
    preceding_blocks = running - block_log
    order = jnp.arange(blocks)
    earlier_mask = order[None, :] < order[:, None]
    relative = preceding_blocks[:, :, None] - running[:, None, :]
    mixing = jnp.where(earlier_mask[None], jnp.exp(jnp.minimum(relative, 0.0)), 0.0)
    local_prefix = jnp.einsum("hcx,xhde->chde", mixing, increments, precision=HIGH)
    own_log = running[:, -1]
    own_state = jnp.einsum(
        "hc,chde->hde", jnp.exp(own_log[:, None] - running), increments, precision=HIGH
    )
    sequence_parts = lax.axis_size("ctx")
    zero_log = jnp.zeros_like(own_log)
    zero_state = jnp.zeros_like(own_state)

    def cycle_step(turn, carry):
        passed = join_states(carry, (own_log, own_state))
        return shifted((passed[0], passed[1]), "ctx", 1)

    prev_log, prev_state = lax.fori_loop(0, sequence_parts - 1, cycle_step, (zero_log, zero_state))
    closing = close_chain(prev_log, prev_state, own_log, own_state, state_in)
    shared_final = broadcast(closing, "ctx", sequence_parts - 1)
    share_rows = width // sequence_parts
    row_start = lax.axis_index("ctx") * share_rows
    final_share = lax.dynamic_slice_in_dim(shared_final, row_start, share_rows, 1)
    incoming_state = jnp.exp(prev_log)[:, None, None] * state_in + prev_state
    starts = jnp.exp(preceding_blocks).T[:, :, None, None] * incoming_state[None] + local_prefix
    starts_low = starts.astype(jnp.bfloat16)
    inter = jnp.einsum("cshd,chde->cshe", q_blocks, starts_low, preferred_element_type=jnp.float32)
    inter = inter * jnp.exp(within).transpose(1, 2, 0)[:, :, :, None]
    attended = (intra + inter).reshape(tokens_here, heads * width)
    squares = lax.psum(jnp.sum(attended * attended, axis=1), "tp")
    scale = lax.rsqrt(squares / (H * DH) + EPSILON)
    normed = (attended * scale[:, None] * norm_gain).astype(jnp.bfloat16)
    partials = jnp.dot(
        normed,
        lax.all_gather(out_weight, "ctx", axis=1, tiled=True),
        preferred_element_type=jnp.float32,
    )
    layer_out = lax.psum_scatter(
        partials.astype(jnp.bfloat16), "tp", scatter_dimension=1, tiled=True
    )
    return (normed, final_share, layer_out)


def solution(mesh):
    return jax.shard_map(
        per_device,
        mesh=mesh,
        in_specs=(
            P("ctx", "tp"),
            P("ctx", "tp"),
            P("ctx", "tp"),
            P("tp", "ctx"),
            P("tp", None, None),
            P("tp"),
            P("tp", "ctx"),
        ),
        out_specs=(P("ctx", "tp"), P("tp", "ctx", None), P("ctx", "tp")),
        check_vma=False,
    )
```

profile of v0, /device:TPU:25, one launch (start us, length us, event | category | flops | bytes accessed | tf_op | source)
XLA Modules:
  0.0 428.5 jit_solution(16179808259684997788)
XLA Ops:
  10.1 2.6 broadcast_multiply_fusion
  12.8 288.8 %while.13 = (s32[]{:T(128)}, f32[16]{0:T(128)S(1)}, f32[16,128,128]{2,1,0:T(8,128)S(1)}, f32[16]{0:T(128)S(1)}, f32[16,1,1]{0,2,1:T(1,128)S(1)}, /*index=5*/f32[16,128,128]{2,1,0:T(8,128)S(1)}, s32[]{:T(128)}) while((s32[]{:T(128)}, f32[16]{0:T(128)S(1)}, f32[16,128,128]{2,1,0:T(8,128)S(1)}, f32[16]{0:T(128)S(1)}, f32[16,1,1]{0,2,1:T(1,128)S(1)}, ...), condition=%wide.region_3.4_spmd, body=%wide.region_2.3_spmd.sunk | while | flops 524306 | bytes 7340701 | solution.py:77
  15.4 1.3 collective-permute-start
  16.7 2.5 collective-permute-done
  21.7 1.3 collective-permute-start
  23.0 39.6 %collective-permute-done = f32[16]{0:T(128)S(1)} collective-permute-done((f32[16]{0:T(128)S(1)}, f32[16]{0:T(128)S(1)}, u32[]{:S(2)}, u32[]{:S(2)}) %collective-permute-start) | collective-permute-done | bytes 96 | tf_op jit(solution)/shard_map/while/body/eval_jaxpr/ppermute | solution.py:18
  65.2 1.3 collective-permute-start
  66.5 65.6 %collective-permute-done = f32[16]{0:T(128)S(1)} collective-permute-done((f32[16]{0:T(128)S(1)}, f32[16]{0:T(128)S(1)}, u32[]{:S(2)}, u32[]{:S(2)}) %collective-permute-start) | collective-permute-done | bytes 96 | tf_op jit(solution)/shard_map/while/body/eval_jaxpr/ppermute | solution.py:18
  134.9 1.3 collective-permute-start
  136.2 59.2 %collective-permute-done = f32[16]{0:T(128)S(1)} collective-permute-done((f32[16]{0:T(128)S(1)}, f32[16]{0:T(128)S(1)}, u32[]{:S(2)}, u32[]{:S(2)}) %collective-permute-start) | collective-permute-done | bytes 96 | tf_op jit(solution)/shard_map/while/body/eval_jaxpr/ppermute | solution.py:18
  197.9 1.3 collective-permute-start
  199.2 58.4 %collective-permute-done = f32[16]{0:T(128)S(1)} collective-permute-done((f32[16]{0:T(128)S(1)}, f32[16]{0:T(128)S(1)}, u32[]{:S(2)}, u32[]{:S(2)}) %collective-permute-start) | collective-permute-done | bytes 96 | tf_op jit(solution)/shard_map/while/body/eval_jaxpr/ppermute | solution.py:18
  260.1 1.3 collective-permute-start
  261.4 22.6 %collective-permute-done = f32[16]{0:T(128)S(1)} collective-permute-done((f32[16]{0:T(128)S(1)}, f32[16]{0:T(128)S(1)}, u32[]{:S(2)}, u32[]{:S(2)}) %collective-permute-start) | collective-permute-done | bytes 96 | tf_op jit(solution)/shard_map/while/body/eval_jaxpr/ppermute | solution.py:18
  287.9 13.8 %collective-permute-done = f32[16]{0:T(128)S(1)} collective-permute-done((f32[16]{0:T(128)S(1)}, f32[16]{0:T(128)S(1)}, u32[]{:S(2)}, u32[]{:S(2)}) %collective-permute-start) | collective-permute-done | bytes 96 | tf_op jit(solution)/shard_map/while/body/eval_jaxpr/ppermute | solution.py:18
  301.7 2.5 add_select_fusion
  304.4 4.7 %fusion.1 = f32[16,256,128]{1,2,0:T(8,128)} fusion(bf16[256,16,128]{0,2,1:T(8,128)(2,1)} %bitcast.75, f32[16,256]{1,0:T(8,128)S(1)} %bitcast_add_fusion, pred[256,256]{1,0:T(8,128)(4,1)S(1)} %iota_compare_fusion, bf16[256,2048]{1,0:T(8,128)(2,1)} %param.11, bf16[256,2048]{1,0:T(8,128)(2,1)S(1)} %copy-done), kind=kOutput, calls=%fused_computation.8 | convolution fusion | flops 542113792 | bytes 5324800 | tf_op jit(solution)/shard_map/hcst,cthd->cshd/dot_general | solution.py:51
  309.1 4.1 multiply_reduce_fusion
  313.2 1.9 copy.43
  315.1 7.9 %psum.14 = f32[256]{0:T(256)S(1)} all-reduce(f32[256]{0:T(256)S(1)} %get-tuple-element.91), channel_id=1, replica_groups=mesh['ctx'=8,'tp'=4] {'tp'}, use_global_device_ids=true, to_apply=%region_5.6 | all-reduce | flops 256 | bytes 2048 | tf_op jit(solution)/shard_map/psum | solution.py:89
  324.3 13.2 %convolution_convert_fusion = bf16[256,6144]{1,0:T(8,128)(2,1)} fusion(bf16[256,2048]{1,0:T(8,128)(2,1)} %multiply_convert_fusion.1, bf16[2048,6144]{1,0:T(8,128)(2,1)} %all-gather.2.cloned.1.call-done), kind=kOutput, calls=%fused_computation.1 | convolution fusion | flops 6444023808 | bytes 29360128 | tf_op jit(solution)/shard_map/dot_general | solution.py:92
  337.5 35.1 %all-reduce.2.cloned.1.call-done = f32[16,128,128]{2,1,0:T(8,128)} async-done(((f32[16,128,128]{2,1,0:T(8,128)}), f32[16,128,128]{2,1,0:T(8,128)}) %all-reduce.2.cloned.1.call-update) | async-done | bytes 1048592 | tf_op jit(solution)/shard_map/psum | solution.py:23
  372.6 1.6 constant_dynamic-slice_fusion
  374.2 47.8 %reduce-scatter.2.cloned.1.call-done = bf16[256,1536]{1,0:T(8,128)(2,1)} async-done(((bf16[256,6144]{1,0:T(8,128)(2,1)}), bf16[256,1536]{1,0:T(8,128)(2,1)}) %reduce-scatter.2.cloned.1.call-update) | async-done | bytes 786448 | tf_op jit(solution)/shard_map/reduce_scatter | solution.py:97
  (73 shorter events, 23.5 us)
Async XLA Ops:
  7.2 297.2 %copy-start = (bf16[256,2048]{1,0:T(8,128)(2,1)S(1)}, bf16[256,2048]{1,0:T(8,128)(2,1)}, u32[]{:S(2)}) copy-start(bf16[256,2048]{1,0:T(8,128)(2,1)} %param.9) | copy-start | bytes 3145732
  7.2 0.8 copy-start.4
  7.2 1.7 copy-start.3
  7.2 317.1 %all-gather.2.cloned.1.call-start = ((), (), s32[]{:S(2)}) async-start(), calls=%async_computation.2 | async-start | bytes 28311552 | tf_op jit(solution)/shard_map/all_gather | solution.py:94
  7.9 364.7 %all-reduce.2.cloned.1.call-start = ((), (), s32[]{:S(2)}) async-start(), calls=%async_computation.1 | async-start | bytes 2097152 | tf_op jit(solution)/shard_map/psum | solution.py:23
  9.4 3.3 copy-start.2
  14.1 5.1 %collective-permute-start.1 = (f32[16,128,128]{2,1,0:T(8,128)}, f32[16,128,128]{2,1,0:T(8,128)S(1)}, u32[]{:S(2)}, u32[]{:S(2)}) collective-permute-start(f32[16,128,128]{2,1,0:T(8,128)} %multiply_add_fusion.2), channel_id=1, source_target_pairs={{0,4},{4,8},{8,12},{12,16},{16,20},{20,24},{24,28},{1,5},{5,9},{9,... | collective-permute-start | bytes 3145736 | tf_op jit(solution)/shard_map/while/body/eval_jaxpr/ppermute | solution.py:18
  15.4 3.8 collective-permute-start
  20.4 42.2 %collective-permute-start.1 = (f32[16,128,128]{2,1,0:T(8,128)}, f32[16,128,128]{2,1,0:T(8,128)S(1)}, u32[]{:S(2)}, u32[]{:S(2)}) collective-permute-start(f32[16,128,128]{2,1,0:T(8,128)} %multiply_add_fusion.2), channel_id=1, source_target_pairs={{0,4},{4,8},{8,12},{12,16},{16,20},{20,24},{24,28},{1,5},{5,9},{9,... | collective-permute-start | bytes 3145736 | tf_op jit(solution)/shard_map/while/body/eval_jaxpr/ppermute | solution.py:18
  21.7 40.9 %collective-permute-start = (f32[16]{0:T(128)S(1)}, f32[16]{0:T(128)S(1)}, u32[]{:S(2)}, u32[]{:S(2)}) collective-permute-start(f32[16]{0:T(128)S(1)} %add.79), channel_id=1, source_target_pairs={{0,4},{4,8},{8,12},{12,16},{16,20},{20,24},{24,28},{1,5},{5,9},{9,... | collective-permute-start | bytes 200 | tf_op jit(solution)/shard_map/while/body/eval_jaxpr/ppermute | solution.py:18
  63.9 68.5 %collective-permute-start.1 = (f32[16,128,128]{2,1,0:T(8,128)}, f32[16,128,128]{2,1,0:T(8,128)S(1)}, u32[]{:S(2)}, u32[]{:S(2)}) collective-permute-start(f32[16,128,128]{2,1,0:T(8,128)} %multiply_add_fusion.2), channel_id=1, source_target_pairs={{0,4},{4,8},{8,12},{12,16},{16,20},{20,24},{24,28},{1,5},{5,9},{9,... | collective-permute-start | bytes 3145736 | tf_op jit(solution)/shard_map/while/body/eval_jaxpr/ppermute | solution.py:18
  65.2 66.9 %collective-permute-start = (f32[16]{0:T(128)S(1)}, f32[16]{0:T(128)S(1)}, u32[]{:S(2)}, u32[]{:S(2)}) collective-permute-start(f32[16]{0:T(128)S(1)} %add.79), channel_id=1, source_target_pairs={{0,4},{4,8},{8,12},{12,16},{16,20},{20,24},{24,28},{1,5},{5,9},{9,... | collective-permute-start | bytes 200 | tf_op jit(solution)/shard_map/while/body/eval_jaxpr/ppermute | solution.py:18
  133.6 61.8 %collective-permute-start.1 = (f32[16,128,128]{2,1,0:T(8,128)}, f32[16,128,128]{2,1,0:T(8,128)S(1)}, u32[]{:S(2)}, u32[]{:S(2)}) collective-permute-start(f32[16,128,128]{2,1,0:T(8,128)} %multiply_add_fusion.2), channel_id=1, source_target_pairs={{0,4},{4,8},{8,12},{12,16},{16,20},{20,24},{24,28},{1,5},{5,9},{9,... | collective-permute-start | bytes 3145736 | tf_op jit(solution)/shard_map/while/body/eval_jaxpr/ppermute | solution.py:18
  134.9 60.5 %collective-permute-start = (f32[16]{0:T(128)S(1)}, f32[16]{0:T(128)S(1)}, u32[]{:S(2)}, u32[]{:S(2)}) collective-permute-start(f32[16]{0:T(128)S(1)} %add.79), channel_id=1, source_target_pairs={{0,4},{4,8},{8,12},{12,16},{16,20},{20,24},{24,28},{1,5},{5,9},{9,... | collective-permute-start | bytes 200 | tf_op jit(solution)/shard_map/while/body/eval_jaxpr/ppermute | solution.py:18
  196.6 61.0 %collective-permute-start.1 = (f32[16,128,128]{2,1,0:T(8,128)}, f32[16,128,128]{2,1,0:T(8,128)S(1)}, u32[]{:S(2)}, u32[]{:S(2)}) collective-permute-start(f32[16,128,128]{2,1,0:T(8,128)} %multiply_add_fusion.2), channel_id=1, source_target_pairs={{0,4},{4,8},{8,12},{12,16},{16,20},{20,24},{24,28},{1,5},{5,9},{9,... | collective-permute-start | bytes 3145736 | tf_op jit(solution)/shard_map/while/body/eval_jaxpr/ppermute | solution.py:18
  197.9 59.7 %collective-permute-start = (f32[16]{0:T(128)S(1)}, f32[16]{0:T(128)S(1)}, u32[]{:S(2)}, u32[]{:S(2)}) collective-permute-start(f32[16]{0:T(128)S(1)} %add.79), channel_id=1, source_target_pairs={{0,4},{4,8},{8,12},{12,16},{16,20},{20,24},{24,28},{1,5},{5,9},{9,... | collective-permute-start | bytes 200 | tf_op jit(solution)/shard_map/while/body/eval_jaxpr/ppermute | solution.py:18
  258.8 25.2 %collective-permute-start.1 = (f32[16,128,128]{2,1,0:T(8,128)}, f32[16,128,128]{2,1,0:T(8,128)S(1)}, u32[]{:S(2)}, u32[]{:S(2)}) collective-permute-start(f32[16,128,128]{2,1,0:T(8,128)} %multiply_add_fusion.2), channel_id=1, source_target_pairs={{0,4},{4,8},{8,12},{12,16},{16,20},{20,24},{24,28},{1,5},{5,9},{9,... | collective-permute-start | bytes 3145736 | tf_op jit(solution)/shard_map/while/body/eval_jaxpr/ppermute | solution.py:18
  260.1 23.9 %collective-permute-start = (f32[16]{0:T(128)S(1)}, f32[16]{0:T(128)S(1)}, u32[]{:S(2)}, u32[]{:S(2)}) collective-permute-start(f32[16]{0:T(128)S(1)} %add.79), channel_id=1, source_target_pairs={{0,4},{4,8},{8,12},{12,16},{16,20},{20,24},{24,28},{1,5},{5,9},{9,... | collective-permute-start | bytes 200 | tf_op jit(solution)/shard_map/while/body/eval_jaxpr/ppermute | solution.py:18
  285.3 16.4 %collective-permute-start.1 = (f32[16,128,128]{2,1,0:T(8,128)}, f32[16,128,128]{2,1,0:T(8,128)S(1)}, u32[]{:S(2)}, u32[]{:S(2)}) collective-permute-start(f32[16,128,128]{2,1,0:T(8,128)} %multiply_add_fusion.2), channel_id=1, source_target_pairs={{0,4},{4,8},{8,12},{12,16},{16,20},{20,24},{24,28},{1,5},{5,9},{9,... | collective-permute-start | bytes 3145736 | tf_op jit(solution)/shard_map/while/body/eval_jaxpr/ppermute | solution.py:18
  286.6 15.1 %collective-permute-start = (f32[16]{0:T(128)S(1)}, f32[16]{0:T(128)S(1)}, u32[]{:S(2)}, u32[]{:S(2)}) collective-permute-start(f32[16]{0:T(128)S(1)} %add.79), channel_id=1, source_target_pairs={{0,4},{4,8},{8,12},{12,16},{16,20},{20,24},{24,28},{1,5},{5,9},{9,... | collective-permute-start | bytes 200 | tf_op jit(solution)/shard_map/while/body/eval_jaxpr/ppermute | solution.py:18
  304.2 117.8 %reduce-scatter.2.cloned.1.call-start = ((), (), s32[]{:S(2)}) async-start(), calls=%async_computation.3 | async-start | bytes 3932160 | tf_op jit(solution)/shard_map/reduce_scatter | solution.py:97
  304.4 4.8 %copy-start.1 = (f32[16,128,128]{2,1,0:T(8,128)S(1)}, f32[16,128,128]{2,1,0:T(8,128)}, u32[]{:S(2)}) copy-start(f32[16,128,128]{2,1,0:T(8,128)} %param.13) | copy-start | bytes 3145732
  313.2 9.9 %copy-start.5 = (f32[2048]{0:T(1024)S(1)}, f32[2048]{0:T(1024)}, u32[]{:S(2)}) copy-start(f32[2048]{0:T(1024)} %param.14) | copy-start | bytes 24580
Sparse Core Ops, SparseCore 0:
  9.6 263.0 all-gather.1
  304.3 68.2 all-reduce.1
  376.2 45.7 reduce-scatter.1
where the time goes:
time: 431 us; the launch traced here: 429 us
  waiting for transfers between devices  346 us (80%)
  matrix products  24.6 us (6%)
  starting transfers between devices  18.1 us (4%)
  between operations  13.9 us (3%)
  other arithmetic  13.3 us (3%)
  blocking collectives  7.9 us (2%)
  local copies, waits for them, and re-layouts  4.91 us (1%)
    ppermute x14, waiting for transfers between devices, shifted(): return lax.ppermute(x, axis, pairs)  262 us
    reduce_scatter x1, waiting for transfers between devices, per_device(): lax.psum_scatter(partials.astype(jnp.bfloat16), 'tp', scatter_dimension=1...  47.8 us
    psum x1, waiting for transfers between devices, broadcast(): return lax.psum(jnp.where(mine, x, jnp.zeros_like(x)), axis)  35.1 us
    ppermute x14, starting transfers between devices, shifted(): return lax.ppermute(x, axis, pairs)  18 us
    dot_general x1, matrix products, per_device(): jnp.dot(normed, lax.all_gather(out_weight, 'ctx', axis=1, tiled=True), pr...  13.2 us
    add x7, other arithmetic, join_states(): jnp.exp(log_late)[:, None, None] * state_early + state_late  8.66 us
  transfers between devices with their start and end apart: 17, of which 10 were waited for; matrix products, arithmetic and copies ran while one was open for 10% of the time, Pallas kernels for 0%

commit v1 on v0

v1 whole, which is shorter than its diff:
```python
import functools

import jax
import jax.numpy as jnp
from jax import lax
from jax.experimental import pallas as pl
from jax.experimental.pallas import tpu as pltpu
from jax.sharding import PartitionSpec as P

EPSILON = 1e-06
HIGH = lax.Precision.HIGHEST
MESH = pl.DeviceIdType.MESH
F32 = jnp.float32
BF16 = jnp.bfloat16


def wait_bytes(ref, sem):
    pltpu.make_async_copy(ref, ref, sem).wait()


def dot(a, b, over, precision=None):
    return lax.dot_general(
        a, b, (over, ((), ())), precision=precision, preferred_element_type=F32
    )


def kernel(
    peers, groups, chunks,
    q, k, v, logs, s_in, gain, w_hbm,
    normed, state, layer,
    w, padded, brow, bcol, inc, zst, att, cin, cout, shares, ssq_out, ssq_in,
    acts, parts, arrived, summed,
    w_sem, chain_s, chain_r, st_s, st_r, sq_s, sq_r, a_s, a_r, rs_s, rs_r, fin_s, fin_r,
):
    c = lax.axis_index("ctx")
    t = lax.axis_index("tp")
    heads, tokens = logs.shape
    width = s_in.shape[1]
    share = state.shape[0] // heads
    chips = peers // 2
    z, j = c // 2, c % 2
    ratio = peers // groups
    rows_here = tokens // groups
    per_chunk = heads // chunks
    last = peers - 1

    def remote(src, dst, send, recv, ctx, tp):
        return pltpu.make_async_remote_copy(
            src_ref=src, dst_ref=dst, send_sem=send, recv_sem=recv,
            device_id={"ctx": ctx, "tp": tp}, device_id_type=MESH,
        )

    w_copy = pltpu.make_async_copy(w_hbm, w, w_sem)
    w_copy.start()
    barrier = pltpu.get_barrier_semaphore()
    everyone = peers * groups

    def greet(i, carry):
        other = (c * groups + t + i) % everyone
        pl.semaphore_signal(
            barrier, inc=1,
            device_id={"ctx": other // groups, "tp": other % groups},
            device_id_type=MESH,
        )
        return carry

    lax.fori_loop(1, everyone, greet, 0)

    padded[...] = jnp.zeros_like(padded)
    padded[0:heads, :] = logs[...]
    rows = lax.broadcasted_iota(jnp.int32, (tokens, tokens), 0)
    cols = lax.broadcasted_iota(jnp.int32, (tokens, tokens), 1)
    upper = jnp.where(rows <= cols, 1.0, 0.0).astype(F32)
    by_row = dot(padded[...], upper, ((1,), (0,)), HIGH)
    brow[...] = by_row
    bcol[...] = by_row.T
    lane = lax.broadcasted_iota(jnp.int32, (tokens, 128), 1)

    def column(h):
        return jnp.sum(jnp.where(lane == h, bcol[...], 0.0), axis=1, keepdims=True)

    def head_cols(h):
        return pl.ds(pl.multiple_of(h * width, width), width)

    def head_increment(h, carry):
        hs = head_cols(h)
        summed_logs = column(h)
        factor = jnp.exp(summed_logs[tokens - 1 : tokens] - summed_logs)
        decayed = (k[:, hs].astype(F32) * factor).astype(BF16)
        inc[h] = dot(decayed, v[:, hs], ((0,), (0,)))
        return carry

    lax.fori_loop(0, heads, head_increment, 0, unroll=min(4, heads))
    pl.semaphore_wait(barrier, everyone - 1)

    def chain_copy(g):
        part = pl.ds(g * per_chunk, per_chunk)
        return remote(cout.at[part], cin.at[part], chain_s.at[g], chain_r.at[g], c + 1, t)

    def pass_on(g, incoming):
        for h in range(g * per_chunk, (g + 1) * per_chunk):
            start = incoming[h].astype(F32)
            zst[h] = start
            end = jnp.exp(brow[h : h + 1, tokens - 1 : tokens]) * start + inc[h]
            cout[h] = end.astype(BF16)

            @pl.when(c == last)
            def _():
                for to in range(peers):
                    shares[to, h * share : (h + 1) * share, :] = end[to * share : (to + 1) * share]

        @pl.when(c < last)
        def _():
            chain_copy(g).start()

    @pl.when(c == 0)
    def _():
        for g in range(chunks):
            pass_on(g, s_in)

    causal = rows >= cols

    def head_intra(h, carry):
        hs = head_cols(h)
        scores = dot(q[:, hs], k[:, hs], ((1,), (1,)))
        spread = jnp.minimum(column(h) - brow[pl.ds(h, 1), :], 0.0)
        weights = (scores * jnp.where(causal, jnp.exp(spread), 0.0)).astype(BF16)
        att[:, hs] = dot(weights, v[:, hs], ((1,), (0,)))
        return carry

    lax.fori_loop(0, heads, head_intra, 0, unroll=min(2, heads))

    @pl.when(c > 0)
    def _():
        for g in range(chunks):
            wait_bytes(cin.at[pl.ds(g * per_chunk, per_chunk)], chain_r.at[g])
            pass_on(g, cin)

    def head_inter(h, squares):
        hs = head_cols(h)
        inter = dot(q[:, hs], zst[h].astype(BF16), ((1,), (0,))) * jnp.exp(column(h))
        whole = att[:, hs] + inter
        att[:, hs] = whole
        return squares + whole * whole

    squares = lax.fori_loop(
        0, heads, head_inter, jnp.zeros((tokens, width), F32), unroll=min(4, heads)
    )
    ssq_out[...] = dot(jnp.ones((8, width), F32), squares, ((1,), (1,)), HIGH)
    for off in range(1, groups):
        remote(ssq_out, ssq_in.at[off - 1], sq_s, sq_r, c, (t + off) % groups).start()
    wait_bytes(ssq_in, sq_r)
    total = ssq_out[...]
    for off in range(1, groups):
        total = total + ssq_in[off - 1]
    spread_total = dot(total, jnp.full((8, width), 0.125, F32), ((0,), (0,)), HIGH)
    scale = lax.rsqrt(spread_total / (groups * heads * width) + EPSILON)

    def head_norm(h, carry):
        hs = head_cols(h)
        out = (att[:, hs] * scale * gain[:, hs]).astype(BF16)
        normed[:, hs] = out
        acts[c, :, hs] = out
        return carry

    lax.fori_loop(0, heads, head_norm, 0, unroll=min(4, heads))

    def up(s):
        return remote(acts.at[s], acts.at[s], a_s.at[0, s], a_r.at[s], c + 2, t)

    def down(s):
        return remote(acts.at[s], acts.at[s], a_s.at[1, s], a_r.at[s], c - 2, t)

    def across(s):
        return remote(acts.at[s], acts.at[s], a_s.at[2, s], a_r.at[s], c + 1 - 2 * j, t)

    def state_copy(to):
        return remote(shares.at[to], state, st_s.at[to], st_r, to, t)

    @pl.when(z < chips - 1)
    def _():
        up(c).start()

    @pl.when(z > 0)
    def _():
        down(c).start()

    across(c).start()

    @pl.when(c == last)
    def _():
        for to in range(last):
            state_copy(to).start()
        state[...] = shares[last]

    def chip_at(i):
        near_end = jnp.minimum(z, chips - 1 - z)
        half = (i + 1) // 2
        near = jnp.where(i % 2 == 1, z - half, z + half)
        far = jnp.where(z < chips - 1 - z, z + (i - near_end), z - (i - near_end))
        return jnp.where(i <= 2 * near_end, near, far)

    def project(s):
        depth = w.shape[1]
        for n in range(0, depth, 256):
            m = min(n + 256, depth)
            parts[s, :, n:m] = dot(acts[s], w[:, n:m], ((1,), (0,))).astype(BF16)
        for off in range(1, groups):
            to = (t + off) % groups
            src = parts.at[s, pl.ds(pl.multiple_of(to * rows_here, rows_here), rows_here)]
            remote(src, arrived.at[s, off - 1], rs_s.at[s], rs_r.at[s], c, to).start()

    own_rows = pl.ds(pl.multiple_of(t * rows_here, rows_here), rows_here)
    home = c // ratio

    def final_copy(s):
        return remote(
            summed.at[s], layer.at[c % ratio, own_rows], fin_s.at[s], fin_r, s, home
        )

    def stays(s):
        return jnp.logical_and(s == c, home == t)

    def finish(s):
        wait_bytes(arrived.at[s], rs_r.at[s])
        added = parts[s, own_rows].astype(F32)
        for off in range(1, groups):
            added = added + arrived[s, off - 1].astype(F32)
        summed[s] = added.astype(BF16)

        @pl.when(stays(s))
        def _():
            pltpu.make_async_copy(summed.at[s], layer.at[c % ratio, own_rows], fin_r).start()

        @pl.when(jnp.logical_not(stays(s)))
        def _():
            final_copy(s).start()

    w_copy.wait()

    def step(i, carry):
        zk = chip_at(i)
        s = 2 * zk + j

        @pl.when(i > 0)
        def _():
            wait_bytes(acts.at[s], a_r.at[s])

            @pl.when(jnp.logical_and(zk < z, z < chips - 1))
            def _():
                up(s).start()

            @pl.when(jnp.logical_and(zk > z, z > 0))
            def _():
                down(s).start()

            across(s).start()

        project(s)
        other = 2 * zk + 1 - j
        wait_bytes(acts.at[other], a_r.at[other])
        project(other)

        @pl.when(i > 0)
        def _():
            before = chip_at(i - 1)
            finish(2 * before + j)
            finish(2 * before + 1 - j)

        return carry

    lax.fori_loop(0, chips, step, 0)
    final_chip = chip_at(chips - 1)
    finish(2 * final_chip + j)
    finish(2 * final_chip + 1 - j)

    wait_bytes(layer, fin_r)
    wait_bytes(ssq_in, sq_s)

    @pl.when(c < last)
    def _():
        wait_bytes(state, st_r)
        for g in range(chunks):
            chain_copy(g).wait_send()

    @pl.when(c == last)
    def _():
        for to in range(last):
            state_copy(to).wait_send()

    def drain_chip(zk, carry):
        s = 2 * zk + j

        @pl.when(jnp.logical_and(zk <= z, z < chips - 1))
        def _():
            up(s).wait_send()

        @pl.when(jnp.logical_and(zk >= z, z > 0))
        def _():
            down(s).wait_send()

        across(s).wait_send()
        return carry

    lax.fori_loop(0, chips, drain_chip, 0)

    def drain_slot(s, carry):
        wait_bytes(arrived.at[s], rs_s.at[s])

        @pl.when(jnp.logical_not(stays(s)))
        def _():
            final_copy(s).wait_send()

        return carry

    lax.fori_loop(0, peers, drain_slot, 0)


def per_device(peers, groups, queries, keys, values, log_keep, state_in, norm_gain, out_weight):
    heads, tokens = log_keep.shape
    width = state_in.shape[1]
    columns = queries.shape[1]
    depth = out_weight.shape[1]
    chunks = min(4, heads)
    share = width // peers
    ratio = peers // groups
    rows_here = tokens // groups
    dma = pltpu.SemaphoreType.DMA
    vmem = pl.BlockSpec(memory_space=pltpu.VMEM)
    normed, state, layer = pl.pallas_call(
        functools.partial(kernel, peers, groups, chunks),
        out_shape=(
            jax.ShapeDtypeStruct((tokens, columns), BF16),
            jax.ShapeDtypeStruct((heads * share, width), F32),
            jax.ShapeDtypeStruct((ratio, tokens, depth), BF16),
        ),
        in_specs=[vmem] * 6 + [pl.BlockSpec(memory_space=pl.ANY)],
        out_specs=(vmem, vmem, vmem),
        scratch_shapes=[
            pltpu.VMEM(out_weight.shape, BF16),
            pltpu.VMEM((128, tokens), F32),
            pltpu.VMEM((128, tokens), F32),
            pltpu.VMEM((tokens, 128), F32),
            pltpu.VMEM((heads, width, width), F32),
            pltpu.VMEM((heads, width, width), F32),
            pltpu.VMEM((tokens, columns), F32),
            pltpu.VMEM((heads, width, width), BF16),
            pltpu.VMEM((heads, width, width), BF16),
            pltpu.VMEM((peers, heads * share, width), F32),
            pltpu.VMEM((8, tokens), F32),
            pltpu.VMEM((groups - 1, 8, tokens), F32),
            pltpu.VMEM((peers, tokens, columns), BF16),
            pltpu.VMEM((peers, tokens, depth), BF16),
            pltpu.VMEM((peers, groups - 1, rows_here, depth), BF16),
            pltpu.VMEM((peers, rows_here, depth), BF16),
            dma,
            dma((chunks,)),
            dma((chunks,)),
            dma((peers,)),
            dma,
            dma,
            dma,
            dma((3, peers)),
            dma((peers,)),
            dma((peers,)),
            dma((peers,)),
            dma((peers,)),
            dma,
        ],
        compiler_params=pltpu.CompilerParams(
            collective_id=0, has_side_effects=True, vmem_limit_bytes=56 * 1024 * 1024
        ),
        name="attend_project",
    )(queries, keys, values, log_keep, state_in, norm_gain[None, :], out_weight)
    state = state.reshape(heads, share, width)
    layer = layer.transpose(1, 0, 2).reshape(tokens, ratio * depth)
    return normed, state, layer


def solution(mesh):
    peers, groups = mesh.shape["ctx"], mesh.shape["tp"]
    return jax.shard_map(
        functools.partial(per_device, peers, groups),
        mesh=mesh,
        in_specs=(
            P("ctx", "tp"),
            P("ctx", "tp"),
            P("ctx", "tp"),
            P("tp", "ctx"),
            P("tp", None, None),
            P("tp"),
            P("tp", "ctx"),
        ),
        out_specs=(P("ctx", "tp"), P("tp", "ctx", None), P("ctx", "tp")),
        check_vma=False,
    )
```

time: 431 us -> 148 us (0.34)
  waiting for transfers between devices: 346 us -> 0 us
  Pallas kernels: 0 us -> 142 us
  matrix products: 24.6 us -> 0 us
  starting transfers between devices: 18.1 us -> 0 us
  other arithmetic: 13.3 us -> 0 us
  between operations: 13.9 us -> 0.66 us
  blocking collectives: 7.9 us -> 0 us
    ppermute x14 -> x0, waiting for transfers between devices: 262 us -> none  [shifted(): return lax.ppermute(x, axis, pairs)]
    pallas_call x0 -> x1, Pallas kernels: none -> 142 us  [per_device(): pl.pallas_call(functools.partial(kernel, peers, groups, chunks), out_shap...]
    reduce_scatter x1 -> x0, waiting for transfers between devices: 47.8 us -> none  [per_device(): lax.psum_scatter(partials.astype(jnp.bfloat16), 'tp', scatter_dimension=1...]
    psum x1 -> x0, waiting for transfers between devices: 35.1 us -> none  [broadcast(): return lax.psum(jnp.where(mine, x, jnp.zeros_like(x)), axis)]
    dot_general x4 -> x0, matrix products: 24.6 us -> none  [the longest x1 13.2 us: per_device(): jnp.dot(normed, lax.all_gather(out_weight, 'ctx', axis=1, tiled=True), pr...]
    ppermute x14 -> x0, starting transfers between devices: 18 us -> none  [shifted(): return lax.ppermute(x, axis, pairs)]
    add x14 -> x0, other arithmetic: 8.69 us -> none  [the longest x7 8.66 us: join_states(): jnp.exp(log_late)[:, None, None] * state_early + state_late]
    psum x1 -> x0, blocking collectives: 7.9 us -> none  [per_device(): squares = lax.psum(jnp.sum(attended * attended, axis=1), 'tp')]
  transfers between devices with their start and end apart: 17 -> 0, of which waited for: 10 -> 0; matrix products, arithmetic and copies ran while one was open for 10% -> 0% of each run, Pallas kernels for 0% -> 0%
where the time goes in v1:
time: 148 us; the launch traced here: 147 us
  Pallas kernels  142 us (96%)
  local copies, waits for them, and re-layouts  4.28 us (3%)
    pallas_call x1, Pallas kernels, per_device(): pl.pallas_call(functools.partial(kernel, peers, groups, chunks), out_shap...  142 us

profile of v1, /device:TPU:25, one launch (start us, length us, event | category | flops | bytes accessed | tf_op | source)
XLA Modules:
  0.0 147.4 jit_solution(7216878482615732925)
XLA Ops:
  0.6 142.5 %attend_project.1 = (bf16[256,2048]{1,0:T(8,128)(2,1)}, f32[256,128]{1,0:T(8,128)}, bf16[2,256,768]{2,1,0:T(8,128)(2,1)}) custom-call(bf16[256,2048]{1,0:T(8,128)(2,1)} %q.1, bf16[256,2048]{1,0:T(8,128)(2,1)} %k.1, bf16[256,2048]{1,0:T(8,128)(2,1)} %v.1, f32[16,256]{1,0:T(8,128)} %logs.1, f32[16,128,128]{2,1,0:T(8,128)} %s_in.1, f32[1,2048]{1,0:T(1,128)} %bitcast.7, ...), custom_call_target="tpu_custom_call" | custom-call | tf_op jit(solution)/shard_map/attend_project/pallas_call | solution.py:330
  143.1 0.0 copy-start
  143.1 0.0 copy-start.1
  143.1 1.5 %copy.10 = bf16[256,2,768]{0,2,1:T(8,128)(2,1)S(1)} copy(bf16[256,2,768]{2,0,1:T(8,128)(2,1)} %bitcast.5) | data formatting | bytes 1572864 | tf_op jit(solution)/shard_map/transpose | solution.py:376
  144.6 1.2 copy.11
  145.8 0.0 copy-done
  145.8 1.0 copy.14
  146.7 0.0 copy-done.1
  146.8 0.7 copy.15
Async XLA Ops:
  143.1 2.7 %copy-start = (bf16[256,2048]{1,0:T(8,128)(2,1)S(1)}, bf16[256,2048]{1,0:T(8,128)(2,1)}, u32[]{:S(2)}) copy-start(bf16[256,2048]{1,0:T(8,128)(2,1)} %get-tuple-element.15) | copy-start | bytes 3145732
  143.1 3.6 %copy-start.1 = (f32[256,128]{1,0:T(8,128)S(1)}, f32[256,128]{1,0:T(8,128)}, u32[]{:S(2)}) copy-start(f32[256,128]{1,0:T(8,128)} %get-tuple-element.7) | copy-start | bytes 393220

commit v2 on v1

--- a/solution.py
+++ b/solution.py
@@ -29,7 +29,7 @@
     q, k, v, logs, s_in, gain, w_hbm,
     normed, state, layer,
     w, padded, brow, bcol, inc, zst, att, cin, cout, shares, ssq_out, ssq_in,
-    acts, parts, arrived, summed,
+    acts, parts, arrived, summed, squares, scale, landed,
     w_sem, chain_s, chain_r, st_s, st_r, sq_s, sq_r, a_s, a_r, rs_s, rs_r, fin_s, fin_r,
 ):
     c = lax.axis_index("ctx")
@@ -136,62 +136,65 @@
             wait_bytes(cin.at[pl.ds(g * per_chunk, per_chunk)], chain_r.at[g])
             pass_on(g, cin)
 
-    def head_inter(h, squares):
-        hs = head_cols(h)
-        inter = dot(q[:, hs], zst[h].astype(BF16), ((1,), (0,))) * jnp.exp(column(h))
-        whole = att[:, hs] + inter
-        att[:, hs] = whole
-        return squares + whole * whole
-
-    squares = lax.fori_loop(
-        0, heads, head_inter, jnp.zeros((tokens, width), F32), unroll=min(4, heads)
-    )
-    ssq_out[...] = dot(jnp.ones((8, width), F32), squares, ((1,), (1,)), HIGH)
+    def up(s, g):
+        return remote(acts.at[s, g], acts.at[s, g], a_s.at[0, s, g], a_r.at[s, g], c + 2, t)
+
+    def down(s, g):
+        return remote(acts.at[s, g], acts.at[s, g], a_s.at[1, s, g], a_r.at[s, g], c - 2, t)
+
+    def across(s, g):
+        return remote(
+            acts.at[s, g], acts.at[s, g], a_s.at[2, s, g], a_r.at[s, g], c + 1 - 2 * j, t
+        )
+
+    def state_copy(to):
+        return remote(shares.at[to], state, st_s.at[to], st_r, to, t)
+
+    squares[...] = jnp.zeros_like(squares)
+    for g in range(chunks):
+        for i in range(per_chunk):
+            h = g * per_chunk + i
+            hs = slice(h * width, (h + 1) * width)
+            inter = dot(q[:, hs], zst[h].astype(BF16), ((1,), (0,))) * jnp.exp(bcol[:, h : h + 1])
+            whole = att[:, hs] + inter
+            att[:, hs] = whole
+            squares[...] += whole * whole
+            acts[c, g, :, i * width : (i + 1) * width] = (whole * gain[:, hs]).astype(BF16)
+
+        @pl.when(z > 0)
+        def _():
+            down(c, g).start()
+
+        across(c, g).start()
+
+    @pl.when(z < chips - 1)
+    def _():
+        for g in range(chunks):
+            up(c, g).start()
+
+    ssq_out[...] = dot(jnp.ones((8, width), F32), squares[...], ((1,), (1,)), HIGH)
     for off in range(1, groups):
         remote(ssq_out, ssq_in.at[off - 1], sq_s, sq_r, c, (t + off) % groups).start()
+
+    @pl.when(c == last)
+    def _():
+        for to in range(last):
+            state_copy(to).start()
+        state[...] = shares[last]
+
     wait_bytes(ssq_in, sq_r)
     total = ssq_out[...]
     for off in range(1, groups):
         total = total + ssq_in[off - 1]
     spread_total = dot(total, jnp.full((8, width), 0.125, F32), ((0,), (0,)), HIGH)
-    scale = lax.rsqrt(spread_total / (groups * heads * width) + EPSILON)
+    scale[...] = lax.rsqrt(spread_total / (groups * heads * width) + EPSILON)
 
     def head_norm(h, carry):
         hs = head_cols(h)
-        out = (att[:, hs] * scale * gain[:, hs]).astype(BF16)
-        normed[:, hs] = out
-        acts[c, :, hs] = out
+        normed[:, hs] = (att[:, hs] * scale[...] * gain[:, hs]).astype(BF16)
         return carry
 
     lax.fori_loop(0, heads, head_norm, 0, unroll=min(4, heads))
-
-    def up(s):
-        return remote(acts.at[s], acts.at[s], a_s.at[0, s], a_r.at[s], c + 2, t)
-
-    def down(s):
-        return remote(acts.at[s], acts.at[s], a_s.at[1, s], a_r.at[s], c - 2, t)
-
-    def across(s):
-        return remote(acts.at[s], acts.at[s], a_s.at[2, s], a_r.at[s], c + 1 - 2 * j, t)
-
-    def state_copy(to):
-        return remote(shares.at[to], state, st_s.at[to], st_r, to, t)
-
-    @pl.when(z < chips - 1)
-    def _():
-        up(c).start()
-
-    @pl.when(z > 0)
-    def _():
-        down(c).start()
-
-    across(c).start()
-
-    @pl.when(c == last)
-    def _():
-        for to in range(last):
-            state_copy(to).start()
-        state[...] = shares[last]
 
     def chip_at(i):
         near_end = jnp.minimum(z, chips - 1 - z)
@@ -202,9 +205,10 @@
 
     def project(s):
         depth = w.shape[1]
+        rows_of = jnp.concatenate([acts[s, g] for g in range(chunks)], axis=1)
         for n in range(0, depth, 256):
             m = min(n + 256, depth)
-            parts[s, :, n:m] = dot(acts[s], w[:, n:m], ((1,), (0,))).astype(BF16)
+            parts[s, :, n:m] = dot(rows_of, w[:, n:m], ((1,), (0,))).astype(BF16)
         for off in range(1, groups):
             to = (t + off) % groups
             src = parts.at[s, pl.ds(pl.multiple_of(to * rows_here, rows_here), rows_here)]
@@ -215,7 +219,7 @@
 
     def final_copy(s):
         return remote(
-            summed.at[s], layer.at[c % ratio, own_rows], fin_s.at[s], fin_r, s, home
+            summed.at[s], landed.at[c % ratio, own_rows], fin_s.at[s], fin_r, s, home
         )
 
     def stays(s):
@@ -230,7 +234,7 @@
 
         @pl.when(stays(s))
         def _():
-            pltpu.make_async_copy(summed.at[s], layer.at[c % ratio, own_rows], fin_r).start()
+            pltpu.make_async_copy(summed.at[s], landed.at[c % ratio, own_rows], fin_r).start()
 
         @pl.when(jnp.logical_not(stays(s)))
         def _():
@@ -244,21 +248,23 @@
 
         @pl.when(i > 0)
         def _():
-            wait_bytes(acts.at[s], a_r.at[s])
-
-            @pl.when(jnp.logical_and(zk < z, z < chips - 1))
-            def _():
-                up(s).start()
-
-            @pl.when(jnp.logical_and(zk > z, z > 0))
-            def _():
-                down(s).start()
-
-            across(s).start()
+            for g in range(chunks):
+                wait_bytes(acts.at[s, g], a_r.at[s, g])
+
+                @pl.when(jnp.logical_and(zk < z, z < chips - 1))
+                def _():
+                    up(s, g).start()
+
+                @pl.when(jnp.logical_and(zk > z, z > 0))
+                def _():
+                    down(s, g).start()
+
+                across(s, g).start()
 
         project(s)
         other = 2 * zk + 1 - j
-        wait_bytes(acts.at[other], a_r.at[other])
+        for g in range(chunks):
+            wait_bytes(acts.at[other, g], a_r.at[other, g])
         project(other)
 
         @pl.when(i > 0)
@@ -274,7 +280,16 @@
     finish(2 * final_chip + j)
     finish(2 * final_chip + 1 - j)
 
-    wait_bytes(layer, fin_r)
+    wait_bytes(landed, fin_r)
+    depth = w.shape[1]
+    for i in range(ratio):
+        for n in range(0, depth, 128):
+            m = min(n + 128, depth)
+            out = (landed[i, :, n:m].astype(F32) * scale[:, 0 : m - n]).astype(BF16)
+            if depth % 128 == 0:
+                layer[:, i * depth + n : i * depth + m] = out
+            else:
+                layer[i, :, n:m] = out
     wait_bytes(ssq_in, sq_s)
 
     @pl.when(c < last)
@@ -293,13 +308,16 @@
 
         @pl.when(jnp.logical_and(zk <= z, z < chips - 1))
         def _():
-            up(s).wait_send()
+            for g in range(chunks):
+                up(s, g).wait_send()
 
         @pl.when(jnp.logical_and(zk >= z, z > 0))
         def _():
-            down(s).wait_send()
-
-        across(s).wait_send()
+            for g in range(chunks):
+                down(s, g).wait_send()
+
+        for g in range(chunks):
+            across(s, g).wait_send()
         return carry
 
     lax.fori_loop(0, chips, drain_chip, 0)
@@ -332,7 +350,9 @@
         out_shape=(
             jax.ShapeDtypeStruct((tokens, columns), BF16),
             jax.ShapeDtypeStruct((heads * share, width), F32),
-            jax.ShapeDtypeStruct((ratio, tokens, depth), BF16),
+            jax.ShapeDtypeStruct(
+                (tokens, ratio * depth) if depth % 128 == 0 else (ratio, tokens, depth), BF16
+            ),
         ),
         in_specs=[vmem] * 6 + [pl.BlockSpec(memory_space=pl.ANY)],
         out_specs=(vmem, vmem, vmem),
@@ -349,10 +369,13 @@
             pltpu.VMEM((peers, heads * share, width), F32),
             pltpu.VMEM((8, tokens), F32),
             pltpu.VMEM((groups - 1, 8, tokens), F32),
-            pltpu.VMEM((peers, tokens, columns), BF16),
+            pltpu.VMEM((peers, chunks, tokens, columns // chunks), BF16),
             pltpu.VMEM((peers, tokens, depth), BF16),
             pltpu.VMEM((peers, groups - 1, rows_here, depth), BF16),
             pltpu.VMEM((peers, rows_here, depth), BF16),
+            pltpu.VMEM((tokens, width), F32),
+            pltpu.VMEM((tokens, width), F32),
+            pltpu.VMEM((ratio, tokens, depth), BF16),
             dma,
             dma((chunks,)),
             dma((chunks,)),
@@ -360,8 +383,8 @@
             dma,
             dma,
             dma,
-            dma((3, peers)),
-            dma((peers,)),
+            dma((3, peers, chunks)),
+            dma((peers, chunks)),
             dma((peers,)),
             dma((peers,)),
             dma((peers,)),
@@ -373,7 +396,8 @@
         name="attend_project",
     )(queries, keys, values, log_keep, state_in, norm_gain[None, :], out_weight)
     state = state.reshape(heads, share, width)
-    layer = layer.transpose(1, 0, 2).reshape(tokens, ratio * depth)
+    if layer.ndim == 3:
+        layer = layer.transpose(1, 0, 2).reshape(tokens, ratio * depth)
     return normed, state, layer
 
 

time: 148 us -> 141 us (0.953)
  the two profiles are of different devices: /device:TPU:25 before, /device:TPU:7 now
where the time goes in v2:
time: 141 us
  Pallas kernels  134 us (95%)
  local copies, waits for them, and re-layouts  5.93 us (4%)
    pallas_call x1, Pallas kernels, per_device(): pl.pallas_call(functools.partial(kernel, peers, groups, chunks), out_shap...  134 us
    unnamed x3, local copies, waits for them, and re-layouts  5.93 us

profile of v2, /device:TPU:7, one launch (start us, length us, event | category | flops | bytes accessed | tf_op | source)
XLA Modules:
  0.0 140.7 jit_solution(7293370975334149622)
XLA Ops:
  0.6 134.1 %attend_project.1 = (bf16[256,2048]{1,0:T(8,128)(2,1)}, f32[256,128]{1,0:T(8,128)}, bf16[256,1536]{1,0:T(8,128)(2,1)}) custom-call(bf16[256,2048]{1,0:T(8,128)(2,1)} %q.1, bf16[256,2048]{1,0:T(8,128)(2,1)} %k.1, bf16[256,2048]{1,0:T(8,128)(2,1)} %v.1, f32[16,256]{1,0:T(8,128)} %logs.1, f32[16,128,128]{2,1,0:T(8,128)} %s_in.1, f32[1,2048]{1,0:T(1,128)} %bitcast.3, ...), custom_call_target="tpu_custom_call" | custom-call | tf_op jit(solution)/shard_map/attend_project/pallas_call | solution.py:348
  134.8 2.3 %copy.13 = bf16[256,2048]{1,0:T(8,128)(2,1)} copy(bf16[256,2048]{1,0:T(8,128)(2,1)} %get-tuple-element.12) | data formatting | bytes 2097152
  137.1 1.6 %copy.14 = f32[16,16,128]{2,1,0:T(8,128)} copy(f32[16,16,128]{2,1,0:T(8,128)} %bitcast.2) | data formatting | bytes 262144
  138.6 2.1 %copy.15 = bf16[256,1536]{1,0:T(8,128)(2,1)} copy(bf16[256,1536]{1,0:T(8,128)(2,1)} %get-tuple-element.14) | data formatting | bytes 1572864

commit v3 on v2

--- a/solution.py
+++ b/solution.py
@@ -29,8 +29,8 @@
     q, k, v, logs, s_in, gain, w_hbm,
     normed, state, layer,
     w, padded, brow, bcol, inc, zst, att, cin, cout, shares, ssq_out, ssq_in,
-    acts, parts, arrived, summed, squares, scale, landed,
-    w_sem, chain_s, chain_r, st_s, st_r, sq_s, sq_r, a_s, a_r, rs_s, rs_r, fin_s, fin_r,
+    acts, parts, arrived, summed, squares, scale, landed, relay,
+    w_sem, chain_s, chain_r, st_s, st_r, sq_s, sq_r, a_s, a_r, rs_s, rs_r, fin_s, mid_r, fwd_s, fin_r,
 ):
     c = lax.axis_index("ctx")
     t = lax.axis_index("tp")
@@ -215,30 +215,44 @@
             remote(src, arrived.at[s, off - 1], rs_s.at[s], rs_r.at[s], c, to).start()
 
     own_rows = pl.ds(pl.multiple_of(t * rows_here, rows_here), rows_here)
-    home = c // ratio
-
-    def final_copy(s):
-        return remote(
-            summed.at[s], landed.at[c % ratio, own_rows], fin_s.at[s], fin_r, s, home
-        )
-
-    def stays(s):
-        return jnp.logical_and(s == c, home == t)
+
+    def to_owner(s):
+        return remote(summed.at[s], relay.at[c], fin_s.at[s], mid_r.at[c], s, t)
 
     def finish(s):
         wait_bytes(arrived.at[s], rs_r.at[s])
         added = parts[s, own_rows].astype(F32)
         for off in range(1, groups):
             added = added + arrived[s, off - 1].astype(F32)
-        summed[s] = added.astype(BF16)
-
-        @pl.when(stays(s))
-        def _():
-            pltpu.make_async_copy(summed.at[s], landed.at[c % ratio, own_rows], fin_r).start()
-
-        @pl.when(jnp.logical_not(stays(s)))
-        def _():
-            final_copy(s).start()
+
+        @pl.when(s == c)
+        def _():
+            relay[c] = added.astype(BF16)
+
+        @pl.when(s != c)
+        def _():
+            summed[s] = added.astype(BF16)
+            to_owner(s).start()
+
+    def to_home(frm):
+        return remote(
+            relay.at[frm], landed.at[frm % ratio, own_rows], fwd_s.at[frm], fin_r, c, frm // ratio
+        )
+
+    def deliver(frm):
+        @pl.when(frm != c)
+        def _():
+            wait_bytes(relay.at[frm], mid_r.at[frm])
+
+        @pl.when(frm // ratio == t)
+        def _():
+            pltpu.make_async_copy(relay.at[frm], landed.at[frm % ratio, own_rows], fin_r).start()
+
+        @pl.when(frm // ratio != t)
+        def _():
+            to_home(frm).start()
+
+    early = chips <= 4
 
     w_copy.wait()
 
@@ -260,25 +274,37 @@
                     down(s, g).start()
 
                 across(s, g).start()
+                if g == 0:
+                    before = chip_at(i - 1)
+                    finish(2 * before + j)
+                    finish(2 * before + 1 - j)
+                    if early:
+
+                        @pl.when(i > 1)
+                        def _():
+                            twice = chip_at(i - 2)
+                            deliver(2 * twice + j)
+                            deliver(2 * twice + 1 - j)
 
         project(s)
         other = 2 * zk + 1 - j
         for g in range(chunks):
             wait_bytes(acts.at[other, g], a_r.at[other, g])
         project(other)
-
-        @pl.when(i > 0)
-        def _():
-            before = chip_at(i - 1)
-            finish(2 * before + j)
-            finish(2 * before + 1 - j)
-
         return carry
 
     lax.fori_loop(0, chips, step, 0)
     final_chip = chip_at(chips - 1)
     finish(2 * final_chip + j)
     finish(2 * final_chip + 1 - j)
+
+    def deliver_chip(i, carry):
+        zk = chip_at(i)
+        deliver(2 * zk + j)
+        deliver(2 * zk + 1 - j)
+        return carry
+
+    lax.fori_loop(max(0, chips - 2) if early else 0, chips, deliver_chip, 0)
 
     wait_bytes(landed, fin_r)
     depth = w.shape[1]
@@ -325,9 +351,13 @@
     def drain_slot(s, carry):
         wait_bytes(arrived.at[s], rs_s.at[s])
 
-        @pl.when(jnp.logical_not(stays(s)))
-        def _():
-            final_copy(s).wait_send()
+        @pl.when(s != c)
+        def _():
+            to_owner(s).wait_send()
+
+        @pl.when(s // ratio != t)
+        def _():
+            to_home(s).wait_send()
 
         return carry
 
@@ -376,6 +406,7 @@
             pltpu.VMEM((tokens, width), F32),
             pltpu.VMEM((tokens, width), F32),
             pltpu.VMEM((ratio, tokens, depth), BF16),
+            pltpu.VMEM((peers, rows_here, depth), BF16),
             dma,
             dma((chunks,)),
             dma((chunks,)),
@@ -385,6 +416,8 @@
             dma,
             dma((3, peers, chunks)),
             dma((peers, chunks)),
+            dma((peers,)),
+            dma((peers,)),
             dma((peers,)),
             dma((peers,)),
             dma((peers,)),
@@ -395,10 +428,27 @@
         ),
         name="attend_project",
     )(queries, keys, values, log_keep, state_in, norm_gain[None, :], out_weight)
-    state = state.reshape(heads, share, width)
     if layer.ndim == 3:
         layer = layer.transpose(1, 0, 2).reshape(tokens, ratio * depth)
-    return normed, state, layer
+    normed, state, layer = write_out(normed, state, layer)
+    return normed, state.reshape(heads, share, width), layer
+
+
+def write_out(*results):
+    def body(*refs):
+        for src, dst in zip(refs[: len(results)], refs[len(results) :]):
+            dst[...] = src[...]
+
+    steps = 4 if all(r.shape[0] % 64 == 0 for r in results) else 2
+    specs = [pl.BlockSpec((r.shape[0] // steps, r.shape[1]), lambda i: (i, 0)) for r in results]
+    return pl.pallas_call(
+        body,
+        grid=(steps,),
+        out_shape=[jax.ShapeDtypeStruct(r.shape, r.dtype) for r in results],
+        in_specs=specs,
+        out_specs=specs,
+        name="write_out",
+    )(*results)
 
 
 def solution(mesh):

time: 141 us -> 139 us (0.986)
  the two profiles are of different devices: /device:TPU:7 before, /device:TPU:25 now
where the time goes in v3:
time: 139 us; the launch traced here: 138 us
  Pallas kernels  137 us (99%)
    pallas_call x1, Pallas kernels, per_device(): pl.pallas_call(functools.partial(kernel, peers, groups, chunks), out_shap...  133 us
    pallas_call x1, Pallas kernels, write_out(): pl.pallas_call(body, grid=(steps,), out_shape=[jax.ShapeDtypeStruct(r.sha...  3.71 us

profile of v3, /device:TPU:25, one launch (start us, length us, event | category | flops | bytes accessed | tf_op | source)
XLA Modules:
  0.0 137.7 jit_solution(12312756573524375223)
XLA Ops:
  0.6 133.3 %attend_project.1 = (bf16[256,2048]{1,0:T(8,128)(2,1)}, f32[256,128]{1,0:T(8,128)}, bf16[256,1536]{1,0:T(8,128)(2,1)}) custom-call(bf16[256,2048]{1,0:T(8,128)(2,1)} %q.1, bf16[256,2048]{1,0:T(8,128)(2,1)} %k.1, bf16[256,2048]{1,0:T(8,128)(2,1)} %v.1, f32[16,256]{1,0:T(8,128)} %logs.1, f32[16,128,128]{2,1,0:T(8,128)} %s_in.1, f32[1,2048]{1,0:T(1,128)} %bitcast.2, ...), custom_call_target="tpu_custom_call" | custom-call | tf_op jit(solution)/shard_map/attend_project/pallas_call | solution.py:378
  134.0 3.7 %write_out.1 = (bf16[256,2048]{1,0:T(8,128)(2,1)}, f32[256,128]{1,0:T(8,128)}, bf16[256,1536]{1,0:T(8,128)(2,1)}) custom-call(bf16[256,2048]{1,0:T(8,128)(2,1)} %get-tuple-element.9.refs_0_, f32[256,128]{1,0:T(8,128)} %get-tuple-element.10.refs_1_, bf16[256,1536]{1,0:T(8,128)(2,1)} %get-tuple-element.11.refs_2_), custom_call_target="tpu_custom_call" | custom-call | tf_op jit(solution)/shard_map/write_out/pallas_call | solution.py:444

commit v4 on v3

--- a/solution.py
+++ b/solution.py
@@ -30,7 +30,9 @@
     normed, state, layer,
     w, padded, brow, bcol, inc, zst, att, cin, cout, shares, ssq_out, ssq_in,
     acts, parts, arrived, summed, squares, scale, landed, relay,
+    w_extra, parts_x, arrived_x, summed_x, relay_x,
     w_sem, chain_s, chain_r, st_s, st_r, sq_s, sq_r, a_s, a_r, rs_s, rs_r, fin_s, mid_r, fwd_s, fin_r,
+    wx_s, wx_r, rsx_s, rsx_r, finx_s, midx_r,
 ):
     c = lax.axis_index("ctx")
     t = lax.axis_index("tp")
@@ -44,6 +46,34 @@
     per_chunk = heads // chunks
     last = peers - 1
 
+    split = chips >= 4 and chunks % 2 == 0
+    kept = chunks // 2
+    half = w.shape[0] // 2
+    at_end = jnp.logical_or(z == 0, z == chips - 1)
+    beside_end = jnp.logical_or(z == 1, z == chips - 2)
+    near_end_chip = jnp.where(z == 1, 0, chips - 1)
+    helped = 2 * near_end_chip + j
+
+    def apart(a, b):
+        return jnp.logical_or(a - b >= 2, b - a >= 2)
+
+    def far(zk):
+        return jnp.logical_and(at_end, apart(zk, z))
+
+    def beyond(zk):
+        return jnp.logical_and(beside_end, apart(zk, near_end_chip))
+
+    def goes(g, zk):
+        return jnp.logical_not(far(zk)) if split and g >= kept else True
+
+    def goes_up(g, zk):
+        limit = chips - 2 if split and g >= kept else chips - 1
+        return jnp.logical_and(zk < z, z < limit)
+
+    def goes_down(g, zk):
+        limit = 1 if split and g >= kept else 0
+        return jnp.logical_and(zk > z, z > limit)
+
     def remote(src, dst, send, recv, ctx, tp):
         return pltpu.make_async_remote_copy(
             src_ref=src, dst_ref=dst, send_sem=send, recv_sem=recv,
@@ -92,6 +122,17 @@
 
     lax.fori_loop(0, heads, head_increment, 0, unroll=min(4, heads))
     pl.semaphore_wait(barrier, everyone - 1)
+
+    def hand_over():
+        return remote(
+            w_hbm.at[pl.ds(half, half)], w_extra, wx_s, wx_r, jnp.where(z == 0, c + 2, c - 2), t
+        )
+
+    if split:
+
+        @pl.when(z == chips - 1)
+        def _():
+            hand_over().start()
 
     def chain_copy(g):
         part = pl.ds(g * per_chunk, per_chunk)
@@ -172,6 +213,12 @@
         for g in range(chunks):
             up(c, g).start()
 
+    if split:
+
+        @pl.when(z == 0)
+        def _():
+            hand_over().start()
+
     ssq_out[...] = dot(jnp.ones((8, width), F32), squares[...], ((1,), (1,)), HIGH)
     for off in range(1, groups):
         remote(ssq_out, ssq_in.at[off - 1], sq_s, sq_r, c, (t + off) % groups).start()
@@ -203,27 +250,62 @@
         far = jnp.where(z < chips - 1 - z, z + (i - near_end), z - (i - near_end))
         return jnp.where(i <= 2 * near_end, near, far)
 
-    def project(s):
-        depth = w.shape[1]
-        rows_of = jnp.concatenate([acts[s, g] for g in range(chunks)], axis=1)
+    depth = w.shape[1]
+
+    def multiply(s, first, end, weights, rows_used, out):
+        rows_of = jnp.concatenate([acts[s, g] for g in range(first, end)], axis=1)
         for n in range(0, depth, 256):
             m = min(n + 256, depth)
-            parts[s, :, n:m] = dot(rows_of, w[:, n:m], ((1,), (0,))).astype(BF16)
+            out[s, :, n:m] = dot(rows_of, weights[0:rows_used, n:m], ((1,), (0,))).astype(BF16)
+
+    def scatter(s, out, into, send, recv):
         for off in range(1, groups):
             to = (t + off) % groups
-            src = parts.at[s, pl.ds(pl.multiple_of(to * rows_here, rows_here), rows_here)]
-            remote(src, arrived.at[s, off - 1], rs_s.at[s], rs_r.at[s], c, to).start()
+            src = out.at[s, pl.ds(pl.multiple_of(to * rows_here, rows_here), rows_here)]
+            remote(src, into.at[s, off - 1], send.at[s], recv.at[s], c, to).start()
+
+    def project(s, zk):
+        if split:
+
+            @pl.when(far(zk))
+            def _():
+                multiply(s, 0, kept, w, half, parts)
+
+            @pl.when(jnp.logical_not(far(zk)))
+            def _():
+                multiply(s, 0, chunks, w, 2 * half, parts)
+
+        else:
+            multiply(s, 0, chunks, w, 2 * half, parts)
+        scatter(s, parts, arrived, rs_s, rs_r)
+
+    def project_extra(s):
+        multiply(s, kept, chunks, w_extra, half, parts_x)
+        scatter(s, parts_x, arrived_x, rsx_s, rsx_r)
 
     own_rows = pl.ds(pl.multiple_of(t * rows_here, rows_here), rows_here)
 
     def to_owner(s):
         return remote(summed.at[s], relay.at[c], fin_s.at[s], mid_r.at[c], s, t)
 
+    def gathered_sum(s, out, into, recv):
+        wait_bytes(into.at[s], recv.at[s])
+        added = out[s, own_rows].astype(F32)
+        for off in range(1, groups):
+            added = added + into[s, off - 1].astype(F32)
+        return added
+
+    def extra_to_owner(s):
+        return remote(
+            summed_x.at[s], relay_x.at[helped], finx_s.at[s], midx_r.at[helped], s, t
+        )
+
+    def finish_extra(s):
+        summed_x[s] = gathered_sum(s, parts_x, arrived_x, rsx_r).astype(BF16)
+        extra_to_owner(s).start()
+
     def finish(s):
-        wait_bytes(arrived.at[s], rs_r.at[s])
-        added = parts[s, own_rows].astype(F32)
-        for off in range(1, groups):
-            added = added + arrived[s, off - 1].astype(F32)
+        added = gathered_sum(s, parts, arrived, rs_r)
 
         @pl.when(s == c)
         def _():
@@ -244,6 +326,16 @@
         def _():
             wait_bytes(relay.at[frm], mid_r.at[frm])
 
+        if split:
+            source = frm // 2
+            from_end = jnp.logical_or(source == 0, source == chips - 1)
+
+            @pl.when(jnp.logical_and(from_end, apart(source, z)))
+            def _():
+                wait_bytes(relay_x.at[frm], midx_r.at[frm])
+                both = relay[frm].astype(F32) + relay_x[frm].astype(F32)
+                relay[frm] = both.astype(BF16)
+
         @pl.when(frm // ratio == t)
         def _():
             pltpu.make_async_copy(relay.at[frm], landed.at[frm % ratio, own_rows], fin_r).start()
@@ -263,17 +355,20 @@
         @pl.when(i > 0)
         def _():
             for g in range(chunks):
-                wait_bytes(acts.at[s, g], a_r.at[s, g])
-
-                @pl.when(jnp.logical_and(zk < z, z < chips - 1))
+
+                @pl.when(goes(g, zk))
+                def _():
+                    wait_bytes(acts.at[s, g], a_r.at[s, g])
+                    across(s, g).start()
+
+                @pl.when(goes_up(g, zk))
                 def _():
                     up(s, g).start()
 
-                @pl.when(jnp.logical_and(zk > z, z > 0))
+                @pl.when(goes_down(g, zk))
                 def _():
                     down(s, g).start()
 
-                across(s, g).start()
                 if g == 0:
                     before = chip_at(i - 1)
                     finish(2 * before + j)
@@ -286,17 +381,48 @@
                             deliver(2 * twice + j)
                             deliver(2 * twice + 1 - j)
 
-        project(s)
+        project(s, zk)
         other = 2 * zk + 1 - j
         for g in range(chunks):
-            wait_bytes(acts.at[other, g], a_r.at[other, g])
-        project(other)
+
+            @pl.when(goes(g, zk))
+            def _():
+                wait_bytes(acts.at[other, g], a_r.at[other, g])
+
+        project(other, zk)
         return carry
 
     lax.fori_loop(0, chips, step, 0)
+    if split:
+
+        @pl.when(beside_end)
+        def _():
+            wait_bytes(w_extra, wx_r)
+
+        def extra_chip(zk, carry):
+            @pl.when(beyond(zk))
+            def _():
+                project_extra(2 * zk)
+                project_extra(2 * zk + 1)
+
+            return carry
+
+        lax.fori_loop(0, chips, extra_chip, 0)
+
     final_chip = chip_at(chips - 1)
     finish(2 * final_chip + j)
     finish(2 * final_chip + 1 - j)
+    if split:
+
+        def extra_sums(zk, carry):
+            @pl.when(beyond(zk))
+            def _():
+                finish_extra(2 * zk)
+                finish_extra(2 * zk + 1)
+
+            return carry
+
+        lax.fori_loop(0, chips, extra_sums, 0)
 
     def deliver_chip(i, carry):
         zk = chip_at(i)
@@ -307,7 +433,6 @@
     lax.fori_loop(max(0, chips - 2) if early else 0, chips, deliver_chip, 0)
 
     wait_bytes(landed, fin_r)
-    depth = w.shape[1]
     for i in range(ratio):
         for n in range(0, depth, 128):
             m = min(n + 128, depth)
@@ -332,19 +457,35 @@
     def drain_chip(zk, carry):
         s = 2 * zk + j
 
-        @pl.when(jnp.logical_and(zk <= z, z < chips - 1))
-        def _():
-            for g in range(chunks):
+        for g in range(chunks):
+
+            @pl.when(jnp.logical_or(goes_up(g, zk), jnp.logical_and(zk == z, z < chips - 1)))
+            def _():
                 up(s, g).wait_send()
 
-        @pl.when(jnp.logical_and(zk >= z, z > 0))
-        def _():
-            for g in range(chunks):
+            @pl.when(jnp.logical_or(goes_down(g, zk), jnp.logical_and(zk == z, z > 0)))
+            def _():
                 down(s, g).wait_send()
 
-        for g in range(chunks):
-            across(s, g).wait_send()
-        return carry
+            @pl.when(goes(g, zk))
+            def _():
+                across(s, g).wait_send()
+
+        if split:
+
+            @pl.when(beyond(zk))
+            def _():
+                for x in (2 * zk, 2 * zk + 1):
+                    wait_bytes(arrived_x.at[x], rsx_s.at[x])
+                    extra_to_owner(x).wait_send()
+
+        return carry
+
+    if split:
+
+        @pl.when(at_end)
+        def _():
+            hand_over().wait_send()
 
     lax.fori_loop(0, chips, drain_chip, 0)
 
@@ -407,6 +548,11 @@
             pltpu.VMEM((tokens, width), F32),
             pltpu.VMEM((ratio, tokens, depth), BF16),
             pltpu.VMEM((peers, rows_here, depth), BF16),
+            pltpu.VMEM((columns // 2, depth), BF16),
+            pltpu.VMEM((peers, tokens, depth), BF16),
+            pltpu.VMEM((peers, groups - 1, rows_here, depth), BF16),
+            pltpu.VMEM((peers, rows_here, depth), BF16),
+            pltpu.VMEM((peers, rows_here, depth), BF16),
             dma,
             dma((chunks,)),
             dma((chunks,)),
@@ -422,6 +568,12 @@
             dma((peers,)),
             dma((peers,)),
             dma,
+            dma,
+            dma,
+            dma((peers,)),
+            dma((peers,)),
+            dma((peers,)),
+            dma((peers,)),
         ],
         compiler_params=pltpu.CompilerParams(
             collective_id=0, has_side_effects=True, vmem_limit_bytes=56 * 1024 * 1024

time: 139 us -> 139 us (level)
  no operation moved by 1% of the time
where the time goes in v4:
time: 139 us
  Pallas kernels  138 us (99%)
    pallas_call x1, Pallas kernels, per_device(): pl.pallas_call(functools.partial(kernel, peers, groups, chunks), out_shap...  134 us
    pallas_call x1, Pallas kernels, write_out(): pl.pallas_call(body, grid=(steps,), out_shape=[jax.ShapeDtypeStruct(r.sha...  3.71 us

profile of v4, /device:TPU:25, one launch (start us, length us, event | category | flops | bytes accessed | tf_op | source)
XLA Modules:
  0.0 138.8 jit_solution(39099723465690086)
XLA Ops:
  0.6 134.4 %attend_project.1 = (bf16[256,2048]{1,0:T(8,128)(2,1)}, f32[256,128]{1,0:T(8,128)}, bf16[256,1536]{1,0:T(8,128)(2,1)}) custom-call(bf16[256,2048]{1,0:T(8,128)(2,1)} %q.1, bf16[256,2048]{1,0:T(8,128)(2,1)} %k.1, bf16[256,2048]{1,0:T(8,128)(2,1)} %v.1, f32[16,256]{1,0:T(8,128)} %logs.1, f32[16,128,128]{2,1,0:T(8,128)} %s_in.1, f32[1,2048]{1,0:T(1,128)} %bitcast.2, ...), custom_call_target="tpu_custom_call" | custom-call | tf_op jit(solution)/shard_map/attend_project/pallas_call | solution.py:519
  135.1 3.7 %write_out.1 = (bf16[256,2048]{1,0:T(8,128)(2,1)}, f32[256,128]{1,0:T(8,128)}, bf16[256,1536]{1,0:T(8,128)(2,1)}) custom-call(bf16[256,2048]{1,0:T(8,128)(2,1)} %get-tuple-element.9.refs_0_, f32[256,128]{1,0:T(8,128)} %get-tuple-element.10.refs_1_, bf16[256,1536]{1,0:T(8,128)(2,1)} %get-tuple-element.11.refs_2_), custom_call_target="tpu_custom_call" | custom-call | tf_op jit(solution)/shard_map/write_out/pallas_call | solution.py:596

commit v5 on v4

--- a/solution.py
+++ b/solution.py
@@ -169,7 +169,20 @@
         att[:, hs] = dot(weights, v[:, hs], ((1,), (0,)))
         return carry
 
-    lax.fori_loop(0, heads, head_intra, 0, unroll=min(2, heads))
+    def intra(g):
+        lax.fori_loop(
+            g * per_chunk, (g + 1) * per_chunk, head_intra, 0, unroll=min(4, per_chunk)
+        )
+
+    sooner = z < chips // 2
+
+    @pl.when(sooner)
+    def _():
+        intra(0)
+
+    @pl.when(jnp.logical_not(sooner))
+    def _():
+        lax.fori_loop(0, heads, head_intra, 0, unroll=min(4, heads))
 
     @pl.when(c > 0)
     def _():
@@ -193,6 +206,12 @@
 
     squares[...] = jnp.zeros_like(squares)
     for g in range(chunks):
+        if g > 0:
+
+            @pl.when(sooner)
+            def _():
+                intra(g)
+
         for i in range(per_chunk):
             h = g * per_chunk + i
             hs = slice(h * width, (h + 1) * width)
@@ -206,18 +225,16 @@
         def _():
             down(c, g).start()
 
+        @pl.when(z == 0)
+        def _():
+            up(c, g).start()
+
         across(c, g).start()
 
-    @pl.when(z < chips - 1)
+    @pl.when(jnp.logical_and(z > 0, z < chips - 1))
     def _():
         for g in range(chunks):
             up(c, g).start()
-
-    if split:
-
-        @pl.when(z == 0)
-        def _():
-            hand_over().start()
 
     ssq_out[...] = dot(jnp.ones((8, width), F32), squares[...], ((1,), (1,)), HIGH)
     for off in range(1, groups):
@@ -347,6 +364,14 @@
     early = chips <= 4
 
     w_copy.wait()
+
+    if split:
+
+        @pl.when(z == 0)
+        def _():
+            for g in range(chunks):
+                up(c, g).wait_send()
+            hand_over().start()
 
     def step(i, carry):
         zk = chip_at(i)
@@ -459,7 +484,14 @@
 
         for g in range(chunks):
 
-            @pl.when(jnp.logical_or(goes_up(g, zk), jnp.logical_and(zk == z, z < chips - 1)))
+            waited = 0 if split else -1
+
+            @pl.when(
+                jnp.logical_or(
+                    goes_up(g, zk),
+                    jnp.logical_and(zk == z, jnp.logical_and(z > waited, z < chips - 1)),
+                )
+            )
             def _():
                 up(s, g).wait_send()
 
@@ -587,18 +619,34 @@
 
 
 def write_out(*results):
+    pieces = []
+    for n, r in enumerate(results):
+        cuts = 4 if r.shape[0] % 64 == 0 and r.dtype == BF16 else 1
+        rows = r.shape[0] // cuts
+        pieces += [(n, i * rows, rows) for i in range(cuts)]
+
     def body(*refs):
-        for src, dst in zip(refs[: len(results)], refs[len(results) :]):
-            dst[...] = src[...]
-
-    steps = 4 if all(r.shape[0] % 64 == 0 for r in results) else 2
-    specs = [pl.BlockSpec((r.shape[0] // steps, r.shape[1]), lambda i: (i, 0)) for r in results]
+        sems = refs[-1]
+        copies = [
+            pltpu.make_async_copy(
+                refs[n].at[pl.ds(first, rows)],
+                refs[len(results) + n].at[pl.ds(first, rows)],
+                sems.at[i],
+            )
+            for i, (n, first, rows) in enumerate(pieces)
+        ]
+        for copy in copies:
+            copy.start()
+        for copy in copies:
+            copy.wait()
+
+    anywhere = [pl.BlockSpec(memory_space=pl.ANY)] * len(results)
     return pl.pallas_call(
         body,
-        grid=(steps,),
         out_shape=[jax.ShapeDtypeStruct(r.shape, r.dtype) for r in results],
-        in_specs=specs,
-        out_specs=specs,
+        in_specs=anywhere,
+        out_specs=anywhere,
+        scratch_shapes=[pltpu.SemaphoreType.DMA((len(pieces),))],
         name="write_out",
     )(*results)
 

time: 139 us -> 195 us (1.40)
  Pallas kernels: 138 us -> 195 us
    pallas_call x1, Pallas kernels: 3.71 us -> 60.7 us  [write_out(): pl.pallas_call(body, out_shape=[jax.ShapeDtypeStruct(r.shape, r.dtype) fo...]
where the time goes in v5:
time: 195 us
  Pallas kernels  195 us (100%)
    pallas_call x1, Pallas kernels, per_device(): pl.pallas_call(functools.partial(kernel, peers, groups, chunks), out_shap...  134 us
    pallas_call x1, Pallas kernels, write_out(): pl.pallas_call(body, out_shape=[jax.ShapeDtypeStruct(r.shape, r.dtype) fo...  60.7 us

profile of v5, /device:TPU:25, one launch (start us, length us, event | category | flops | bytes accessed | tf_op | source)
XLA Modules:
  0.0 195.2 jit_solution(16744716634778648542)
XLA Ops:
  0.6 133.9 %attend_project.1 = (bf16[256,2048]{1,0:T(8,128)(2,1)}, f32[256,128]{1,0:T(8,128)}, bf16[256,1536]{1,0:T(8,128)(2,1)}) custom-call(bf16[256,2048]{1,0:T(8,128)(2,1)} %q.1, bf16[256,2048]{1,0:T(8,128)(2,1)} %k.1, bf16[256,2048]{1,0:T(8,128)(2,1)} %v.1, f32[16,256]{1,0:T(8,128)} %logs.1, f32[16,128,128]{2,1,0:T(8,128)} %s_in.1, f32[1,2048]{1,0:T(1,128)} %bitcast.2, ...), custom_call_target="tpu_custom_call" | custom-call | tf_op jit(solution)/shard_map/attend_project/pallas_call | solution.py:551
  134.5 60.7 %write_out.1 = (bf16[256,2048]{1,0:T(8,128)(2,1)}, f32[256,128]{1,0:T(8,128)}, bf16[256,1536]{1,0:T(8,128)(2,1)}) custom-call(bf16[256,2048]{1,0:T(8,128)(2,1)} %get-tuple-element.9.refs_0_, f32[256,128]{1,0:T(8,128)} %get-tuple-element.10.refs_1_, bf16[256,1536]{1,0:T(8,128)(2,1)} %get-tuple-element.11.refs_2_), custom_call_target="tpu_custom_call" | custom-call | tf_op jit(solution)/shard_map/write_out/pallas_call | solution.py:644

commit v6 on v5

--- a/solution.py
+++ b/solution.py
@@ -364,6 +364,7 @@
     early = chips <= 4
 
     w_copy.wait()
+    first_extra = jnp.where(z == 1, 3, 2)
 
     if split:
 
@@ -406,6 +407,18 @@
                             deliver(2 * twice + j)
                             deliver(2 * twice + 1 - j)
 
+        if split:
+            ahead = chip_at(i - 1)
+
+            @pl.when(jnp.logical_and(beside_end, i == first_extra))
+            def _():
+                wait_bytes(w_extra, wx_r)
+
+            @pl.when(jnp.logical_and(i >= first_extra, beyond(ahead)))
+            def _():
+                project_extra(2 * ahead + j)
+                project_extra(2 * ahead + 1 - j)
+
         project(s, zk)
         other = 2 * zk + 1 - j
         for g in range(chunks):
@@ -418,36 +431,37 @@
         return carry
 
     lax.fori_loop(0, chips, step, 0)
+    final_chip = chip_at(chips - 1)
+
+    def extra_sums(zk):
+        finish_extra(2 * zk + j)
+        finish_extra(2 * zk + 1 - j)
+
     if split:
 
-        @pl.when(beside_end)
-        def _():
-            wait_bytes(w_extra, wx_r)
-
-        def extra_chip(zk, carry):
+        @pl.when(beyond(final_chip))
+        def _():
+            project_extra(2 * final_chip + j)
+            project_extra(2 * final_chip + 1 - j)
+
+        def extra_chip(i, carry):
+            zk = chip_at(i)
+
             @pl.when(beyond(zk))
             def _():
-                project_extra(2 * zk)
-                project_extra(2 * zk + 1)
+                extra_sums(zk)
 
             return carry
 
-        lax.fori_loop(0, chips, extra_chip, 0)
-
-    final_chip = chip_at(chips - 1)
+        lax.fori_loop(0, chips - 1, extra_chip, 0)
+
     finish(2 * final_chip + j)
     finish(2 * final_chip + 1 - j)
     if split:
 
-        def extra_sums(zk, carry):
-            @pl.when(beyond(zk))
-            def _():
-                finish_extra(2 * zk)
-                finish_extra(2 * zk + 1)
-
-            return carry
-
-        lax.fori_loop(0, chips, extra_sums, 0)
+        @pl.when(beyond(final_chip))
+        def _():
+            extra_sums(final_chip)
 
     def deliver_chip(i, carry):
         zk = chip_at(i)
@@ -626,19 +640,29 @@
         pieces += [(n, i * rows, rows) for i in range(cuts)]
 
     def body(*refs):
-        sems = refs[-1]
-        copies = [
-            pltpu.make_async_copy(
-                refs[n].at[pl.ds(first, rows)],
-                refs[len(results) + n].at[pl.ds(first, rows)],
-                sems.at[i],
+        held, sems = refs[2 * len(results) : -1], refs[-1]
+
+        def part(n, i):
+            first, rows = pieces[i][1:]
+            return refs[n].at[pl.ds(first, rows)]
+
+        def inward(i):
+            n, first, rows = pieces[i]
+            return pltpu.make_async_copy(part(n, i), held[n].at[pl.ds(first, rows)], sems.at[0, i])
+
+        def outward(i):
+            n, first, rows = pieces[i]
+            return pltpu.make_async_copy(
+                held[n].at[pl.ds(first, rows)], part(len(results) + n, i), sems.at[1, i]
             )
-            for i, (n, first, rows) in enumerate(pieces)
-        ]
-        for copy in copies:
-            copy.start()
-        for copy in copies:
-            copy.wait()
+
+        for i in range(len(pieces)):
+            inward(i).start()
+        for i in range(len(pieces)):
+            inward(i).wait()
+            outward(i).start()
+        for i in range(len(pieces)):
+            outward(i).wait()
 
     anywhere = [pl.BlockSpec(memory_space=pl.ANY)] * len(results)
     return pl.pallas_call(
@@ -646,7 +670,9 @@
         out_shape=[jax.ShapeDtypeStruct(r.shape, r.dtype) for r in results],
         in_specs=anywhere,
         out_specs=anywhere,
-        scratch_shapes=[pltpu.SemaphoreType.DMA((len(pieces),))],
+        scratch_shapes=[pltpu.VMEM(r.shape, r.dtype) for r in results]
+        + [pltpu.SemaphoreType.DMA((2, len(pieces)))],
+        compiler_params=pltpu.CompilerParams(vmem_limit_bytes=56 * 1024 * 1024),
         name="write_out",
     )(*results)
 

time: 195 us -> 136 us (0.70)
  Pallas kernels: 195 us -> 135 us
    pallas_call x1, Pallas kernels: 60.7 us -> 2.37 us  [write_out(): pl.pallas_call(body, out_shape=[jax.ShapeDtypeStruct(r.shape, r.dtype) fo...]
where the time goes in v6:
time: 136 us
  Pallas kernels  135 us (99%)
    pallas_call x1, Pallas kernels, per_device(): pl.pallas_call(functools.partial(kernel, peers, groups, chunks), out_shap...  133 us

profile of v6, /device:TPU:25, one launch (start us, length us, event | category | flops | bytes accessed | tf_op | source)
XLA Modules:
  0.0 135.6 jit_solution(13837889061383036039)
XLA Ops:
  0.6 132.6 %attend_project.1 = (bf16[256,2048]{1,0:T(8,128)(2,1)}, f32[256,128]{1,0:T(8,128)}, bf16[256,1536]{1,0:T(8,128)(2,1)}) custom-call(bf16[256,2048]{1,0:T(8,128)(2,1)} %q.1, bf16[256,2048]{1,0:T(8,128)(2,1)} %k.1, bf16[256,2048]{1,0:T(8,128)(2,1)} %v.1, f32[16,256]{1,0:T(8,128)} %logs.1, f32[16,128,128]{2,1,0:T(8,128)} %s_in.1, f32[1,2048]{1,0:T(1,128)} %bitcast.2, ...), custom_call_target="tpu_custom_call" | custom-call | tf_op jit(solution)/shard_map/attend_project/pallas_call | solution.py:565
  133.2 2.4 %write_out.1 = (bf16[256,2048]{1,0:T(8,128)(2,1)}, f32[256,128]{1,0:T(8,128)}, bf16[256,1536]{1,0:T(8,128)(2,1)}) custom-call(bf16[256,2048]{1,0:T(8,128)(2,1)} %get-tuple-element.9.refs_0_, f32[256,128]{1,0:T(8,128)} %get-tuple-element.10.refs_1_, bf16[256,1536]{1,0:T(8,128)(2,1)} %get-tuple-element.11.refs_2_), custom_call_target="tpu_custom_call" | custom-call | tf_op jit(solution)/shard_map/write_out/pallas_call | solution.py:668

commit v7 on v6

--- a/solution.py
+++ b/solution.py
@@ -130,7 +130,7 @@
 
     if split:
 
-        @pl.when(z == chips - 1)
+        @pl.when(at_end)
         def _():
             hand_over().start()
 
@@ -365,14 +365,6 @@
 
     w_copy.wait()
     first_extra = jnp.where(z == 1, 3, 2)
-
-    if split:
-
-        @pl.when(z == 0)
-        def _():
-            for g in range(chunks):
-                up(c, g).wait_send()
-            hand_over().start()
 
     def step(i, carry):
         zk = chip_at(i)
@@ -498,12 +490,10 @@
 
         for g in range(chunks):
 
-            waited = 0 if split else -1
-
             @pl.when(
                 jnp.logical_or(
                     goes_up(g, zk),
-                    jnp.logical_and(zk == z, jnp.logical_and(z > waited, z < chips - 1)),
+                    jnp.logical_and(zk == z, z < chips - 1),
                 )
             )
             def _():

time: 136 us -> 169 us (1.24)
  Pallas kernels: 135 us -> 167 us
    pallas_call x1, Pallas kernels: 133 us -> 165 us  [per_device(): pl.pallas_call(functools.partial(kernel, peers, groups, chunks), out_shap...]
where the time goes in v7:
time: 169 us; the launch traced here: 168 us
  Pallas kernels  167 us (99%)
    pallas_call x1, Pallas kernels, per_device(): pl.pallas_call(functools.partial(kernel, peers, groups, chunks), out_shap...  165 us

profile of v7, /device:TPU:25, one launch (start us, length us, event | category | flops | bytes accessed | tf_op | source)
XLA Modules:
  0.0 168.1 jit_solution(16764450597843227924)
XLA Ops:
  0.6 165.1 %attend_project.1 = (bf16[256,2048]{1,0:T(8,128)(2,1)}, f32[256,128]{1,0:T(8,128)}, bf16[256,1536]{1,0:T(8,128)(2,1)}) custom-call(bf16[256,2048]{1,0:T(8,128)(2,1)} %q.1, bf16[256,2048]{1,0:T(8,128)(2,1)} %k.1, bf16[256,2048]{1,0:T(8,128)(2,1)} %v.1, f32[16,256]{1,0:T(8,128)} %logs.1, f32[16,128,128]{2,1,0:T(8,128)} %s_in.1, f32[1,2048]{1,0:T(1,128)} %bitcast.2, ...), custom_call_target="tpu_custom_call" | custom-call | tf_op jit(solution)/shard_map/attend_project/pallas_call | solution.py:555
  165.7 2.4 %write_out.1 = (bf16[256,2048]{1,0:T(8,128)(2,1)}, f32[256,128]{1,0:T(8,128)}, bf16[256,1536]{1,0:T(8,128)(2,1)}) custom-call(bf16[256,2048]{1,0:T(8,128)(2,1)} %get-tuple-element.9.refs_0_, f32[256,128]{1,0:T(8,128)} %get-tuple-element.10.refs_1_, bf16[256,1536]{1,0:T(8,128)(2,1)} %get-tuple-element.11.refs_2_), custom_call_target="tpu_custom_call" | custom-call | tf_op jit(solution)/shard_map/write_out/pallas_call | solution.py:658
